TPU v7x, 128 devices: a whole 4x4x4 slice. The times are simulated.
128 devices in a mesh: wide: 64 (over x, z, y_lo, core), narrow: 2 (over y_hi).
Axes of the slice: x: 4, y: 4 (y_hi: 2, y_lo: 2; y = y_hi * 2 + y_lo), z: 4, core: 2. Of those that a mesh axis runs over, the one named last changes fastest.
Arguments:
- dosage: bfloat16 [2048, 131072], P(None, 'wide'), may hold values from -4 to 6, as said below
- annotations: int32 [128, 131072], P(None, 'wide'), may hold values from 0 to 1, as said below
- test_statistic_table: float32 [131072, 512], P('wide', 'narrow'), may hold values from 0 to 200
Outputs:
- ld_scores: float32 [128, 131072], P(None, ('wide', 'narrow'))
- fitted: float32 [131072, 512], P('wide', 'narrow')
Inputs may be any that keep to these rules, and one draw needn't show every extreme that they name: `dosage`: dosages of each variant follow a correlated process along the variants. `annotations`: 1 where a variant belongs to an annotation.
All inputs are finite; a program needn't handle non-finite values.
Results may differ from a plain program's by a relative error of at most 0.0023.
Values may be sent and summed in bfloat16 or wider, within the bound.
A program may use at most 128 MiB of HBM per device.

v0:
```python
import jax
import jax.numpy as jnp
from jax import lax
from jax.sharding import PartitionSpec as P

HALF = 1024
highest_precision = lax.Precision.HIGHEST


def extended_2(cells, sides, width):
    for axis, dim in sides:
        count = lax.axis_size(axis)
        ends = count - 1
        head = lax.slice_in_dim(cells, 0, width, axis=dim)
        tail = lax.slice_in_dim(cells, cells.shape[dim] - width, cells.shape[dim], axis=dim)
        cells = jnp.concatenate(
            [
                lax.ppermute(tail, axis, [(i, (i + 1) % count) for i in range(ends)]),
                cells,
                lax.ppermute(head, axis, [((i + 1) % count, i) for i in range(ends)]),
            ],
            axis=dim,
        )
    return cells


def band_weights(col_geno, row_geno, col_start, row_start, total_variants):
    products = lax.dot_general(
        col_geno, row_geno, (((0,), (0,)), ((), ())), preferred_element_type=jnp.float32
    )
    samples = row_geno.shape[0]
    correlation = products / samples
    squared = correlation * correlation
    adjusted = squared - (1.0 - squared) / (samples - 2)
    col_index = col_start + jnp.arange(col_geno.shape[1], dtype=jnp.int32)[:, None]
    row_index = row_start + jnp.arange(row_geno.shape[1], dtype=jnp.int32)[None, :]
    inside = (
        (jnp.abs(row_index - col_index) <= HALF) & (col_index >= 0) & (col_index < total_variants)
    )
    return jnp.where(inside, adjusted, 0.0).astype(jnp.bfloat16)


def shards(dosage, annotations, test_statistic_table):
    samples = dosage.shape[0]
    strip_cols = dosage.shape[1]
    half_width = strip_cols // 2
    total_variants = lax.axis_size("wide") * strip_cols
    wide_index = lax.axis_index("wide")
    narrow_index = lax.axis_index("narrow")
    values = dosage.astype(jnp.float32)
    average = jnp.mean(values, axis=0)
    centred_values = values - average[None, :]
    variance = jnp.mean(centred_values * centred_values, axis=0)
    standard = (centred_values / jnp.sqrt(variance + 1e-05)[None, :]).astype(jnp.bfloat16)
    counts = lax.psum(jnp.sum(annotations.astype(jnp.float32), axis=1), "wide")
    shares = counts / total_variants
    centred = (annotations.astype(jnp.float32) - shares[:, None]).astype(jnp.bfloat16)
    stacked = jnp.concatenate([standard, centred], axis=0)
    row_local = narrow_index * half_width
    strip_start = wide_index * strip_cols
    row_start = strip_start + row_local
    own_rows = lax.dynamic_slice_in_dim(standard, row_local, half_width, 1)
    extended = extended_2(stacked, (("wide", 1),), half_width)
    scores = jnp.zeros((centred.shape[0], half_width), jnp.float32)
    for offset in range(3):
        col_block = lax.dynamic_slice_in_dim(
            extended, row_local + offset * half_width, half_width, 1
        )
        weights = band_weights(
            col_block[:samples],
            own_rows,
            row_start - half_width + offset * half_width,
            row_start,
            total_variants,
        )
        scores = scores + jnp.dot(col_block[samples:], weights, preferred_element_type=jnp.float32)
    strip_scores = lax.all_gather(scores, "narrow", axis=1, tiled=True)
    chi_local = jnp.sum(test_statistic_table, axis=0)
    totals = lax.psum(jnp.sum(strip_scores, axis=1), "wide")
    score_mean = totals / total_variants
    deviation = strip_scores - score_mean[:, None]
    cross_local = lax.dot_general(
        deviation,
        deviation,
        (((1,), (1,)), ((), ())),
        precision=highest_precision,
        preferred_element_type=jnp.float32,
    )
    proj_local = jnp.dot(
        deviation,
        test_statistic_table,
        precision=highest_precision,
        preferred_element_type=jnp.float32,
    )
    cross_sum, proj_sum, dev_sum, chi_sum = lax.psum(
        (cross_local, proj_local, jnp.sum(deviation, axis=1), chi_local), "wide"
    )
    chi_mean = chi_sum / total_variants
    covariance = cross_sum / total_variants
    centred_proj = (
        proj_sum / total_variants - (dev_sum / total_variants)[:, None] * chi_mean[None, :]
    )
    spread = jnp.sqrt(jnp.diagonal(covariance) + 1e-05)
    gram_matrix = covariance / (spread[:, None] * spread[None, :])
    projection = centred_proj / spread[:, None]
    factor = jnp.linalg.cholesky(gram_matrix)
    coefficient = jax.scipy.linalg.cho_solve((factor, True), projection)
    standard_scores = (strip_scores - score_mean[:, None]) / spread[:, None]
    fitted = chi_mean[None, :] + lax.dot_general(
        standard_scores,
        coefficient,
        (((0,), (0,)), ((), ())),
        precision=highest_precision,
        preferred_element_type=jnp.float32,
    )
    own_scores = lax.dynamic_slice_in_dim(standard_scores, row_local, half_width, 1)
    return (own_scores, fitted)


def solution(mesh):
    in_specs = (P(None, "wide"), P(None, "wide"), P("wide", "narrow"))
    out_specs = (P(None, ("wide", "narrow")), P("wide", "narrow"))
    return jax.shard_map(shards, mesh=mesh, in_specs=in_specs, out_specs=out_specs, check_vma=False)
```

profile of v0, /device:TPU:0, one launch (start us, length us, event | category | flops | bytes accessed | tf_op | source)
XLA Modules:
  0.0 1175.0 jit_solution(18052722490963843743)
XLA Ops:
  7.2 0.0 all-gather.2.cloned.1.call-start
  7.2 0.0 copy-start
  7.2 4.9 convert_reduce_fusion
  12.2 0.8 copy-done
  13.0 2.2 fusion.2
  15.2 0.0 copy-start.3
  15.2 10.0 fusion.3
  25.2 0.0 copy-done.3
  25.2 0.2 convert_reduce_fusion.1
  25.4 145.3 %psum.42 = f32[128]{0:T(128)S(1)} all-reduce(f32[128]{0:T(128)S(1)} %convert_reduce_fusion.1), channel_id=1, replica_groups=mesh['wide'=64,'narrow'=2] {'wide'}, use_global_device_ids=true, to_apply=%region_3.0 | all-reduce | flops 128 | bytes 1024 | tf_op jit(solution)/shard_map/psum | solution.py:55
  170.7 0.2 subtract_convert_fusion
  170.9 12.3 %fusion.4 = (bf16[2176,1024]{1,0:T(8,128)(2,1)}, bf16[2176,1024]{1,0:T(8,128)(2,1)}) fusion(bf16[2048,2048]{1,0:T(8,128)(2,1)} %fusion.3, bf16[128,2048]{1,0:T(8,128)(2,1)S(1)} %subtract_convert_fusion), kind=kLoop, calls=%fused_computation.10 | loop fusion | flops 17825792 | bytes 17825792 | tf_op jit(solution)/shard_map/concatenate | solution.py:58
  183.2 1.3 collective-permute-start.1
  184.5 5.2 collective-permute-start
  189.8 3.2 collective-permute-done.1
  193.0 2.1 collective-permute-done
  195.0 23.0 %pad_maximum_fusion = bf16[2176,4096]{1,0:T(8,128)(2,1)} fusion(bf16[2176,1024]{1,0:T(8,128)(2,1)} %collective-permute-done.1, bf16[128,2048]{1,0:T(8,128)(2,1)S(1)} %subtract_convert_fusion, bf16[2048,2048]{1,0:T(8,128)(2,1)} %fusion.3, bf16[2176,1024]{1,0:T(8,128)(2,1)} %collective-permute-done), kind=kLoop, calls=%fused_computation.5 | loop fusion | flops 71303168 | bytes 35651584 | tf_op jit(solution)/shard_map/concatenate | solution.py:16
  218.1 10.2 fusion.39
  228.2 11.2 fusion.44
  239.4 0.0 copy-start.2
  239.4 11.1 fusion.52
  250.5 0.0 all-gather.2.cloned.1.call-update
  250.5 0.0 all-reduce.4.cloned.1.call-start
  250.6 106.2 %all-gather.2.cloned.1.call-done = f32[128,2048]{1,0:T(8,128)} async-done(((f32[128,1024]{1,0:T(8,128)}), f32[128,2048]{1,0:T(8,128)}) %all-gather.2.cloned.1.call-update) | async-done | bytes 1048592 | tf_op jit(solution)/shard_map/all_gather | solution.py:77
  356.8 0.0 copy-start.1
  356.8 1.4 reduce_sum.57
  358.2 143.0 %psum.43 = f32[128]{0:T(128)S(1)} all-reduce(f32[128]{0:T(128)S(1)} %reduce_sum.57), channel_id=1, replica_groups=mesh['wide'=64,'narrow'=2] {'wide'}, use_global_device_ids=true, to_apply=%region_5.6 | all-reduce | flops 128 | bytes 1024 | tf_op jit(solution)/shard_map/psum | solution.py:79
  501.2 3.3 fusion.59
  504.5 0.0 copy-done.2
  504.5 3.1 fusion.57
  507.6 0.0 all-reduce.4.cloned.1.call-update
  507.6 0.3 reduce_sum.58
  507.9 488.1 %all-reduce.4.cloned.1.call-done = (f32[128,128]{0,1:T(8,128)}, f32[128,256]{1,0:T(8,128)}) async-done(((f32[128,128]{0,1:T(8,128)}, f32[128,256]{1,0:T(8,128)}), (f32[128,128]{0,1:T(8,128)}, f32[128,256]{1,0:T(8,128)})) %all-reduce.4.cloned.1.call-update) | async-done | bytes 196624 | tf_op jit(solution)/shard_map/psum | solution.py:95
  996.0 0.0 copy-start.4
  996.0 0.9 broadcast_multiply_fusion
  996.9 1.3 gather_fusion
  998.2 0.9 multiply_divide_fusion
  999.1 0.0 copy-done.1
  999.1 0.3 subtract_reduce_fusion
  999.4 0.8 constant_dynamic-slice_fusion
  1000.2 0.1 copy.8
  1000.3 0.9 fusion.75
  1001.3 11.7 cholesky.16
  1013.0 0.6 compare_reduce_fusion
  1013.7 0.7 fusion.71
  1014.3 9.8 custom-call.10
  1024.2 139.8 %all-reduce = (f32[256]{0:T(256)S(1)}, f32[128]{0:T(128)S(1)}) all-reduce(f32[256]{0:T(256)S(1)} %reduce_sum.58, f32[128]{0:T(128)S(1)} %get-tuple-element.8), channel_id=1, replica_groups=mesh['wide'=64,'narrow'=2] {'wide'}, use_global_device_ids=true, to_apply=%region_8.9 | all-reduce | flops 384 | bytes 3072 | tf_op jit(solution)/shard_map/psum | solution.py:95
  1164.0 0.0 copy-done.4
  1164.0 0.4 fusion.66
  1164.4 0.3 fusion.72
  1164.7 3.2 convolution_add_fusion
  (14 shorter events, 0.1 us)
Async XLA Ops:
  7.2 349.6 %all-gather.2.cloned.1.call-start = ((), (), s32[]{:S(2)}) async-start(), calls=%async_computation | async-start | bytes 1572864 | tf_op jit(solution)/shard_map/all_gather | solution.py:77
  7.2 5.8 copy-start
  15.2 10.0 copy-start.3
  183.2 9.8 collective-permute-start.1
  184.5 10.5 collective-permute-start
  239.4 265.1 %copy-start.2 = (f32[2048,256]{1,0:T(8,128)S(1)}, f32[2048,256]{1,0:T(8,128)}, u32[]{:S(2)}) copy-start(f32[2048,256]{1,0:T(8,128)} %param.5) | copy-start | bytes 6291460
  250.5 745.5 %all-reduce.4.cloned.1.call-start = ((), (), s32[]{:S(2)}) async-start(), calls=%async_computation.1 | async-start | bytes 393216 | tf_op jit(solution)/shard_map/psum | solution.py:95
  356.8 642.4 %copy-start.1 = (f32[128,2048]{1,0:T(8,128)S(1)}, f32[128,2048]{1,0:T(8,128)}, u32[]{:S(2)}) copy-start(f32[128,2048]{1,0:T(8,128)} %all-gather.2.cloned.1.call-done) | copy-start | bytes 3145732
  996.0 168.0 %copy-start.4 = (f32[128,256]{1,0:T(8,128)S(1)}, f32[128,256]{1,0:T(8,128)}, u32[]{:S(2)}) copy-start(f32[128,256]{1,0:T(8,128)} %get-tuple-element.5) | copy-start | bytes 393220
Sparse Core Ops, SparseCore 0:
  250.7 106.0 all-gather.1
  507.7 488.2 all-reduce.3
where the time goes:
time: 1180 us
  waiting for transfers between devices  600 us (51%)
  blocking collectives  428 us (36%)
  other arithmetic  80.5 us (7%)
  matrix products  42.6 us (4%)
  between operations  14.6 us (1%)
    psum x1, waiting for transfers between devices, shards(): lax.psum((cross_local, proj_local, jnp.sum(deviation, axis=1), chi_local)...  488 us
    psum x1, blocking collectives, shards(): counts = lax.psum(jnp.sum(annotations.astype(jnp.float32), axis=1), 'wide')  145 us
    psum x1, blocking collectives, shards(): totals = lax.psum(jnp.sum(strip_scores, axis=1), 'wide')  143 us
    psum x1, blocking collectives, shards(): lax.psum((cross_local, proj_local, jnp.sum(deviation, axis=1), chi_local)...  140 us
    all_gather x1, waiting for transfers between devices, shards(): strip_scores = lax.all_gather(scores, 'narrow', axis=1, tiled=True)  106 us
    dot_general x3, matrix products, shards(): jnp.dot(col_block[samples:], weights, preferred_element_type=jnp.float32)  32.5 us
  transfers between devices with their start and end apart: 4, of which 4 were waited for; matrix products, arithmetic and copies ran while one was open for 0% of the time, Pallas kernels for 0%

commit v1 on v0

--- a/solution.py
+++ b/solution.py
@@ -74,7 +74,10 @@
             total_variants,
         )
         scores = scores + jnp.dot(col_block[samples:], weights, preferred_element_type=jnp.float32)
-    strip_scores = lax.all_gather(scores, "narrow", axis=1, tiled=True)
+    devices = lax.axis_size("narrow")
+    tiles = jnp.stack([scores for _ in range(devices)])
+    tiles = lax.all_to_all(tiles, "narrow", split_axis=0, concat_axis=0)
+    strip_scores = jnp.concatenate(tiles, axis=1)
     chi_local = jnp.sum(test_statistic_table, axis=0)
     totals = lax.psum(jnp.sum(strip_scores, axis=1), "wide")
     score_mean = totals / total_variants

time: 1180 us -> 1160 us (0.983)
  waiting for transfers between devices: 600 us -> 507 us
  blocking collectives: 428 us -> 499 us
    all_gather x1 -> x0, waiting for transfers between devices: 106 us -> none  [shards(): strip_scores = lax.all_gather(scores, 'narrow', axis=1, tiled=True)]
    psum x1, blocking collectives: 143 us -> 215 us  [shards(): totals = lax.psum(jnp.sum(strip_scores, axis=1), 'wide')]
    all_to_all x0 -> x1, waiting for transfers between devices: none -> 14.2 us  [shards(): tiles = lax.all_to_all(tiles, 'narrow', split_axis=0, concat_axis=0)]
where the time goes in v1:
time: 1160 us
  waiting for transfers between devices  507 us (44%)
  blocking collectives  499 us (43%)
  other arithmetic  81.2 us (7%)
  matrix products  40.4 us (3%)
  between operations  14.5 us (1%)
    psum x1, waiting for transfers between devices, shards(): lax.psum((cross_local, proj_local, jnp.sum(deviation, axis=1), chi_local)...  488 us
    psum x1, blocking collectives, shards(): totals = lax.psum(jnp.sum(strip_scores, axis=1), 'wide')  215 us
    psum x1, blocking collectives, shards(): counts = lax.psum(jnp.sum(annotations.astype(jnp.float32), axis=1), 'wide')  145 us
    psum x1, blocking collectives, shards(): lax.psum((cross_local, proj_local, jnp.sum(deviation, axis=1), chi_local)...  139 us
    dot_general x3, matrix products, shards(): jnp.dot(col_block[samples:], weights, preferred_element_type=jnp.float32)  30.7 us
  transfers between devices with their start and end apart: 4, of which 4 were waited for; matrix products, arithmetic and copies ran while one was open for 0% of the time, Pallas kernels for 0%

profile of v1, /device:TPU:0, one launch (start us, length us, event | category | flops | bytes accessed | tf_op | source)
XLA Modules:
  0.0 1155.9 jit_solution(7762758721864435997)
XLA Ops:
  7.2 0.0 copy-start
  7.2 4.9 convert_reduce_fusion
  12.1 0.8 copy-done
  12.9 2.2 fusion.2
  15.2 0.0 copy-start.1
  15.2 10.0 fusion.3
  25.2 0.0 copy-done.1
  25.2 0.2 convert_reduce_fusion.1
  25.4 145.3 %psum.42 = f32[128]{0:T(128)S(1)} all-reduce(f32[128]{0:T(128)S(1)} %convert_reduce_fusion.1), channel_id=1, replica_groups=mesh['wide'=64,'narrow'=2] {'wide'}, use_global_device_ids=true, to_apply=%region_3.0 | all-reduce | flops 128 | bytes 1024 | tf_op jit(solution)/shard_map/psum | solution.py:55
  170.7 0.2 subtract_convert_fusion
  170.8 12.3 %fusion.4 = (bf16[2176,1024]{1,0:T(8,128)(2,1)}, bf16[2176,1024]{1,0:T(8,128)(2,1)}) fusion(bf16[2048,2048]{1,0:T(8,128)(2,1)} %fusion.3, bf16[128,2048]{1,0:T(8,128)(2,1)S(1)} %subtract_convert_fusion), kind=kLoop, calls=%fused_computation.10 | loop fusion | flops 17825792 | bytes 17825792 | tf_op jit(solution)/shard_map/concatenate | solution.py:58
  183.2 1.3 collective-permute-start.1
  184.5 5.5 collective-permute-start
  190.0 2.9 collective-permute-done.1
  192.9 2.1 collective-permute-done
  195.0 23.0 %pad_maximum_fusion = bf16[2176,4096]{1,0:T(8,128)(2,1)} fusion(bf16[2176,1024]{1,0:T(8,128)(2,1)} %collective-permute-done.1, bf16[128,2048]{1,0:T(8,128)(2,1)S(1)} %subtract_convert_fusion, bf16[2048,2048]{1,0:T(8,128)(2,1)} %fusion.3, bf16[2176,1024]{1,0:T(8,128)(2,1)} %collective-permute-done), kind=kLoop, calls=%fused_computation.5 | loop fusion | flops 71303168 | bytes 35651584 | tf_op jit(solution)/shard_map/concatenate | solution.py:16
  218.0 10.1 fusion.39
  228.2 10.3 fusion.44
  238.5 10.2 fusion.57
  248.7 1.1 pad_maximum_fusion.2
  249.8 4.2 all-to-all-start
  254.0 0.0 all-reduce.4.cloned.1.call-start
  254.0 1.9 reduce_sum.58
  255.8 14.2 %all-to-all-done = f32[2,128,1024]{2,1,0:T(8,128)S(1)} async-done(((f32[2,128,1024]{2,1,0:T(8,128)}), f32[2,128,1024]{2,1,0:T(8,128)S(1)}, u32[]{:S(2)}, u32[]{:S(2)}) %all-to-all-start) | async-done | bytes 1048608 | tf_op jit(solution)/shard_map/all_to_all | solution.py:79
  270.1 0.1 reduce_sum.57
  270.2 214.7 %psum.43 = f32[128]{0:T(128)S(1)} all-reduce(f32[128]{0:T(128)S(1)} %reduce_sum.57), channel_id=1, replica_groups=mesh['wide'=64,'narrow'=2] {'wide'}, use_global_device_ids=true, to_apply=%region_5.6 | all-reduce | flops 128 | bytes 1024 | tf_op jit(solution)/shard_map/psum | solution.py:82
  484.9 0.3 copy.7
  485.2 0.1 bitcast_subtract_fusion
  485.3 4.2 fusion.110
  489.5 0.2 subtract_reduce_fusion
  489.7 138.6 %all-reduce = (f32[256]{0:T(256)S(1)}, f32[128]{0:T(128)S(1)}) all-reduce(f32[256]{0:T(256)S(1)} %reduce_sum.58, f32[128]{0:T(128)S(1)} %subtract_reduce_fusion), channel_id=1, replica_groups=mesh['wide'=64,'narrow'=2] {'wide'}, use_global_device_ids=true, to_apply=%region_8.9 | all-reduce | flops 384 | bytes 3072 | tf_op jit(solution)/shard_map/psum | solution.py:98
  628.4 1.8 convolution_bitcast_fusion
  630.1 0.0 all-reduce.4.cloned.1.call-update
  630.2 487.5 %all-reduce.4.cloned.1.call-done = (f32[128,128]{0,1:T(8,128)}, f32[128,256]{1,0:T(8,128)}) async-done(((f32[128,128]{0,1:T(8,128)}, f32[128,256]{1,0:T(8,128)}), (f32[128,128]{0,1:T(8,128)}, f32[128,256]{1,0:T(8,128)})) %all-reduce.4.cloned.1.call-update) | async-done | bytes 196624 | tf_op jit(solution)/shard_map/psum | solution.py:98
  1117.7 0.0 copy-start.2
  1117.7 0.0 copy-start.3
  1117.7 0.9 broadcast_multiply_fusion
  1118.6 1.3 gather_fusion
  1119.9 0.1 broadcast_divide_fusion
  1120.0 0.9 multiply_divide_fusion
  1121.0 1.0 copy.10
  1122.0 0.1 copy.9
  1122.1 0.0 copy-done.2
  1122.1 0.1 fusion.76
  1122.2 11.7 %cholesky.16 = f32[128,128]{1,0:T(8,128)S(1)} custom-call(f32[128,128]{1,0:T(8,128)S(1)} %fusion.76), custom_call_target="Cholesky" | custom-call | tf_op jit(solution)/shard_map/jit(cholesky)/cholesky | solution.py:109
  1133.9 0.6 compare_reduce_fusion
  1134.6 0.7 fusion.72
  1135.2 9.8 custom-call.10
  1145.0 0.0 copy-done.3
  1145.1 0.4 fusion.67
  1145.4 0.3 fusion.73
  1145.7 3.1 convolution_add_fusion
  (15 shorter events, 0.2 us)
Async XLA Ops:
  7.2 5.8 copy-start
  15.2 10.0 copy-start.1
  183.2 9.8 collective-permute-start.1
  184.5 10.5 collective-permute-start
  249.8 20.3 %all-to-all-start = ((f32[2,128,1024]{2,1,0:T(8,128)}), f32[2,128,1024]{2,1,0:T(8,128)S(1)}, u32[]{:S(2)}, u32[]{:S(2)}) async-start(f32[2,128,1024]{2,1,0:T(8,128)} %pad_maximum_fusion.2), calls=%async_computation | async-start | bytes 2097152 | tf_op jit(solution)/shard_map/all_to_all | solution.py:79
  254.0 863.7 %all-reduce.4.cloned.1.call-start = ((), (), s32[]{:S(2)}) async-start(), calls=%async_computation.1 | async-start | bytes 393216 | tf_op jit(solution)/shard_map/psum | solution.py:98
  1117.7 4.4 copy-start.2
  1117.7 27.4 %copy-start.3 = (f32[128,256]{1,0:T(8,128)S(1)}, f32[128,256]{1,0:T(8,128)}, u32[]{:S(2)}) copy-start(f32[128,256]{1,0:T(8,128)} %get-tuple-element.7) | copy-start | bytes 393220
Sparse Core Ops, SparseCore 0:
  630.3 487.3 all-reduce.3
